TPU v7x, 32 devices: a whole 2x2x4 slice. The times are simulated.
32 devices in a mesh: space: 4 (over z), rows: 4 (over y, core), cols: 2 (over x).
Axes of the slice: x: 2, y: 2, z: 4, core: 2. Of those that a mesh axis runs over, the one named last changes fastest.
Arguments:
- occupation: float32 [12288, 2048], P(('cols', 'rows'), 'space'), may hold values from -13.5 to 13.5, as said below
- propagator: float32 [12288, 12288], P('rows', 'cols'), may hold values from -0.5 to 1, as said below
- flags_first: int32 [12288, 2048], P(('cols', 'rows'), 'space'), may hold values from 0 to 2
- flags_second: int32 [12288, 2048], P(('rows', 'cols'), 'space'), may hold values from 0 to 2
- courant: float32 [12288], replicated, may hold values from -0.9 to 0.9
- weights: float32 [12288], replicated, may hold values from 0.5 to 6
Outputs:
- occupation_out: float32 [12288, 2048], P(('cols', 'rows'), 'space')
- temperature: float32 [2048], P('space')
Inputs may be any that keep to these rules, and one draw needn't show every extreme that they name: occupation varies from mode to mode and cell to cell. propagator equals its transpose.
All inputs are finite; a program needn't handle non-finite values.
Results may differ from a plain program's by a relative error of at most 0.0003.
Values sent between devices are 32-bit elements; how exact they have to be, the bound alone decides.
A program may use at most 192 MiB of HBM per device.

v0:
```python
import jax
import jax.numpy as jnp
from jax import lax
from jax.sharding import PartitionSpec as P

highest = lax.Precision.HIGHEST


def padded_2(block, sides, width):
    for axis, dim in sides:
        count = lax.axis_size(axis)
        forward = [(i, i + 1) for i in range(count - 1)]
        backward = [(target, source) for source, target in forward]
        low = lax.ppermute(
            lax.slice_in_dim(block, block.shape[dim] - width, None, axis=dim), axis, forward
        )
        high = lax.ppermute(lax.slice_in_dim(block, 0, width, axis=dim), axis, backward)
        block = jnp.concatenate([low, block, high], axis=dim)
    return block


def limited(left_diff, right_diff, selector):
    left_size = jnp.abs(left_diff)
    right_size = jnp.abs(right_diff)
    agreement = 0.5 * (jnp.sign(left_diff) + jnp.sign(right_diff))
    minmod_size = jnp.minimum(left_size, right_size)
    central_size = jnp.minimum(2.0 * minmod_size, 0.5 * jnp.abs(left_diff + right_diff))
    superbee_size = jnp.maximum(
        jnp.minimum(2.0 * left_size, right_size), jnp.minimum(left_size, 2.0 * right_size)
    )
    chosen = jnp.where(
        selector == 0.0, minmod_size, jnp.where(selector == 1.0, central_size, superbee_size)
    )
    return agreement * chosen


def advect(padded, selector, courant_col):
    differences = padded[:, 1:] - padded[:, :-1]
    slopes = limited(differences[:, :-1], differences[:, 1:], selector[:, 1:-1])
    centers = padded[:, 1:-1]
    forward = courant_col * (centers[:, :-1] + 0.5 * (1.0 - courant_col) * slopes[:, :-1])
    backward = courant_col * (centers[:, 1:] - 0.5 * (1.0 + courant_col) * slopes[:, 1:])
    fluxes = jnp.where(courant_col > 0.0, forward, backward)
    return padded[:, 2:-2] - (fluxes[:, 1:] - fluxes[:, :-1])


def advect_slab(field, selector, courant_part):
    stacked = jnp.stack([field, selector.astype(jnp.float32)])
    padded = padded_2(stacked, (("space", 2),), 2)
    return advect(padded[0], padded[1], courant_part[:, None])


def heat_all(weight_part, shifted):
    return lax.psum(jnp.dot(weight_part, shifted, precision=highest), ("rows", "cols"))


def on_device(occupation, propagator, flags_first, flags_second, courant, weights):
    row_count = lax.axis_size("rows")
    col_count = lax.axis_size("cols")
    row_index = lax.axis_index("rows")
    col_index = lax.axis_index("cols")
    local_modes = occupation.shape[0]
    weight_total = jnp.sum(weights)
    offset_first = (col_index * row_count + row_index) * local_modes
    weight_first = lax.dynamic_slice_in_dim(weights, offset_first, local_modes)
    courant_first = lax.dynamic_slice_in_dim(courant, offset_first, local_modes)
    shifted = advect_slab(occupation, flags_first, courant_first)
    heat = heat_all(weight_first, shifted) / weight_total
    deviation = shifted - weight_first[:, None] * heat[None, :]
    partial_value = jnp.dot(
        propagator,
        lax.all_gather(deviation, "rows", axis=0, tiled=True),
        precision=highest,
        preferred_element_type=jnp.float32,
    )
    summed = lax.psum_scatter(partial_value, "cols", scatter_dimension=0, tiled=True)
    offset_second = (row_index * col_count + col_index) * local_modes
    weight_second = lax.dynamic_slice_in_dim(weights, offset_second, local_modes)
    courant_second = lax.dynamic_slice_in_dim(courant, offset_second, local_modes)
    middle = summed + weight_second[:, None] * heat[None, :]
    shifted_second = advect_slab(middle, flags_second, courant_second)
    heat_second = heat_all(weight_second, shifted_second) / weight_total
    deviation_second = shifted_second - weight_second[:, None] * heat_second[None, :]
    partial_second = lax.dot_general(
        propagator,
        lax.all_gather(deviation_second, "cols", axis=0, tiled=True),
        (((0,), (0,)), ((), ())),
        precision=highest,
        preferred_element_type=jnp.float32,
    )
    final = lax.psum_scatter(partial_second, "rows", scatter_dimension=0, tiled=True)
    final = final + weight_first[:, None] * heat_second[None, :]
    return (final, heat_second)


def solution(mesh):
    placed = (
        P(("cols", "rows"), "space"),
        P("rows", "cols"),
        P(("cols", "rows"), "space"),
        P(("rows", "cols"), "space"),
        P(),
        P(),
    )
    return jax.shard_map(
        on_device,
        mesh=mesh,
        in_specs=placed,
        out_specs=(P(("cols", "rows"), "space"), P("space")),
        check_vma=False,
    )
```

profile of v0, /device:TPU:0, one launch (start us, length us, event | category | flops | bytes accessed | tf_op | source)
XLA Modules:
  0.0 710.0 jit_solution(4095584417497403205)
XLA Ops:
  7.2 3.5 copy.9
  10.8 2.1 convert_bitcast_fusion.1
  12.9 3.5 copy.8
  17.3 4.9 collective-permute-start
  25.1 2.8 collective-permute-done.1
  27.9 2.4 pad_maximum_fusion
  31.2 4.0 select_multiply_fusion.1
  35.2 1.4 fusion.7
  36.5 1.7 copy-done.1
  38.2 3.1 fusion.12
  41.3 13.4 %psum.14 = f32[512]{0:T(512)S(1)} all-reduce(f32[512]{0:T(512)S(1)} %bitcast.29), channel_id=1, replica_groups=mesh['space'=4,'rows'=4,'cols'=2] {'rows','cols'}, use_global_device_ids=true, to_apply=%region_0.0 | all-reduce | flops 512 | bytes 4096 | tf_op jit(solution)/shard_map/psum | solution.py:54
  55.3 5.7 multiply_subtract_fusion.1
  61.3 81.5 %all-gather.3.cloned.1.call-done = f32[6144,512]{0,1:T(8,128)} async-done(((f32[1536,512]{0,1:T(8,128)}), f32[6144,512]{0,1:T(8,128)}) %all-gather.3.cloned.1.call-update) | async-done | bytes 12582928 | tf_op jit(solution)/shard_map/all_gather | solution.py:72
  142.8 128.0 %convolution_bitcast_fusion.1 = f32[3072,512]{0,1:T(8,128)} fusion(f32[6144,512]{0,1:T(8,128)} %all-gather.3.cloned.1.call-done, f32[3072,6144]{1,0:T(8,128)} %param.7), kind=kOutput, calls=%fused_computation.3 | convolution fusion | flops 115964116992 | bytes 94371840 | tf_op jit(solution)/shard_map/dot_general | solution.py:70
  270.9 1.8 copy-done.2
  272.7 2.4 copy.10
  275.1 2.2 convert_bitcast_fusion
  277.3 70.8 %reduce-scatter.3.cloned.1.call-done = f32[1536,512]{0,1:T(8,128)} async-done(((f32[3072,512]{0,1:T(8,128)}), f32[1536,512]{0,1:T(8,128)}) %reduce-scatter.3.cloned.1.call-update) | async-done | bytes 3145744 | tf_op jit(solution)/shard_map/reduce_scatter | solution.py:76
  348.1 2.2 add_bitcast_fusion
  350.3 3.4 collective-permute-start.2
  353.7 1.5 collective-permute-start.3
  355.3 4.2 collective-permute-done.3
  361.3 4.0 select_multiply_fusion
  366.7 1.7 copy-done
  368.3 3.1 fusion.14
  371.4 12.4 %psum.15 = f32[512]{0:T(512)S(1)} all-reduce(f32[512]{0:T(512)S(1)} %bitcast.30), channel_id=1, replica_groups=mesh['space'=4,'rows'=4,'cols'=2] {'rows','cols'}, use_global_device_ids=true, to_apply=%region_3.4 | all-reduce | flops 512 | bytes 4096 | tf_op jit(solution)/shard_map/psum | solution.py:54
  384.5 5.7 multiply_subtract_fusion
  390.6 80.4 %all-gather.5.cloned.1.call-done = f32[3072,512]{0,1:T(8,128)} async-done(((f32[1536,512]{0,1:T(8,128)}), f32[3072,512]{0,1:T(8,128)}) %all-gather.5.cloned.1.call-update) | async-done | bytes 6291472 | tf_op jit(solution)/shard_map/all_gather | solution.py:86
  471.0 128.6 %convolution_bitcast_fusion = f32[6144,512]{0,1:T(8,128)} fusion(f32[3072,512]{0,1:T(8,128)} %all-gather.5.cloned.1.call-done, f32[3072,6144]{1,0:T(8,128)} %param.7), kind=kOutput, calls=%fused_computation | convolution fusion | flops 115964116992 | bytes 94371840 | tf_op jit(solution)/shard_map/dot_general | solution.py:84
  599.7 99.2 %reduce-scatter.5.cloned.1.call-done = f32[1536,512]{0,1:T(8,128)} async-done(((f32[6144,512]{0,1:T(8,128)}), f32[1536,512]{0,1:T(8,128)}) %reduce-scatter.5.cloned.1.call-update) | async-done | bytes 3145744 | tf_op jit(solution)/shard_map/reduce_scatter | solution.py:91
  698.9 2.2 multiply_add_fusion
  701.1 2.4 copy.11
  (35 shorter events, 9.8 us)
Async XLA Ops:
  7.2 135.7 %all-gather.3.cloned.1.call-start = ((), (), s32[]{:S(2)}) async-start(), calls=%async_computation.2 | async-start | bytes 15728640 | tf_op jit(solution)/shard_map/all_gather | solution.py:72
  16.4 8.0 %copy-start.3 = (f32[12288]{0:T(1024)S(1)}, f32[12288]{0:T(1024)}, u32[]{:S(2)}) copy-start(f32[12288]{0:T(1024)} %param.11) | copy-start | bytes 147460
  17.3 7.8 %collective-permute-start = (f32[2,1536,2]{1,2,0:T(2,128)S(1)}, f32[2,1536,2]{1,2,0:T(2,128)S(1)}, u32[]{:S(2)}, u32[]{:S(2)}) collective-permute-start(f32[2,1536,2]{1,2,0:T(2,128)S(1)} %get-tuple-element.14), channel_id=1, source_target_pairs={{0,8},{8,16},{16,24},{1,9},{9,17},{17,25},{2,10},{10,18},{18,26},{... | collective-permute-start | bytes 73736 | tf_op jit(solution)/shard_map/ppermute | solution.py:14
  22.2 5.7 collective-permute-start.1
  36.5 1.7 copy-start.1
  61.1 287.0 %reduce-scatter.3.cloned.1.call-start = ((), (), s32[]{:S(2)}) async-start(), calls=%async_computation.3 | async-start | bytes 9437184 | tf_op jit(solution)/shard_map/reduce_scatter | solution.py:76
  270.8 1.9 copy-start.2
  270.8 200.2 %all-gather.5.cloned.1.call-start = ((), (), s32[]{:S(2)}) async-start(), calls=%async_computation.4 | async-start | bytes 9437184 | tf_op jit(solution)/shard_map/all_gather | solution.py:86
  350.3 4.9 collective-permute-start.2
  353.7 5.7 collective-permute-start.3
  366.6 1.7 copy-start
  384.5 314.4 %copy-start.4 = (f32[512]{0:T(512)}, f32[512]{0:T(512)S(1)}, u32[]{:S(2)}) copy-start(f32[512]{0:T(512)S(1)} %broadcast_divide_fusion) | copy-start | bytes 6148
  390.2 308.6 %reduce-scatter.5.cloned.1.call-start = ((), (), s32[]{:S(2)}) async-start(), calls=%async_computation.5 | async-start | bytes 15728640 | tf_op jit(solution)/shard_map/reduce_scatter | solution.py:91
Sparse Core Ops, SparseCore 0:
  61.2 81.6 all-gather.2
  271.0 77.0 reduce-scatter.2
  390.4 80.5 all-gather.4
  599.8 99.0 reduce-scatter.4
where the time goes:
time: 711 us; the launch traced here: 710 us
  waiting for transfers between devices  339 us (48%)
  matrix products  263 us (37%)
  other arithmetic  38.7 us (5%)
  blocking collectives  25.8 us (4%)
  local copies, waits for them, and re-layouts  18 us (3%)
  between operations  14 us (2%)
  starting transfers between devices  11.7 us (2%)
    dot_general x1, matrix products, on_device(): lax.dot_general(propagator, lax.all_gather(deviation_second, 'cols', axis...  129 us
    dot_general x1, matrix products, on_device(): jnp.dot(propagator, lax.all_gather(deviation, 'rows', axis=0, tiled=True)...  128 us
    reduce_scatter x1, waiting for transfers between devices, on_device(): lax.psum_scatter(partial_second, 'rows', scatter_dimension=0, tiled=True)  99.2 us
    all_gather x1, waiting for transfers between devices, on_device(): lax.all_gather(deviation, 'rows', axis=0, tiled=True)  81.5 us
    all_gather x1, waiting for transfers between devices, on_device(): lax.all_gather(deviation_second, 'cols', axis=0, tiled=True)  80.4 us
    reduce_scatter x1, waiting for transfers between devices, on_device(): lax.psum_scatter(partial_value, 'cols', scatter_dimension=0, tiled=True)  70.8 us
    psum x2, blocking collectives, heat_all(): lax.psum(jnp.dot(weight_part, shifted, precision=highest), ('rows', 'cols'))  25.8 us
    unnamed x14, local copies, waits for them, and re-layouts  17 us
  transfers between devices with their start and end apart: 8, of which 6 were waited for; matrix products, arithmetic and copies ran while one was open for 1% of the time, Pallas kernels for 0%

commit v1 on v0

v1 whole, which is shorter than its diff:
```python
import jax
import jax.numpy as jnp
from jax import lax
from jax.sharding import PartitionSpec as P

highest = lax.Precision.HIGHEST
high = lax.Precision.HIGH
CHUNKS = (2, 2)


def padded_2(block, sides, width):
    for axis, dim in sides:
        count = lax.axis_size(axis)
        forward = [(i, i + 1) for i in range(count - 1)]
        backward = [(target, source) for source, target in forward]
        low = lax.ppermute(
            lax.slice_in_dim(block, block.shape[dim] - width, None, axis=dim), axis, forward
        )
        high = lax.ppermute(lax.slice_in_dim(block, 0, width, axis=dim), axis, backward)
        block = jnp.concatenate([low, block, high], axis=dim)
    return block


def limited(left_diff, right_diff, selector):
    left_size = jnp.abs(left_diff)
    right_size = jnp.abs(right_diff)
    agreement = 0.5 * (jnp.sign(left_diff) + jnp.sign(right_diff))
    minmod_size = jnp.minimum(left_size, right_size)
    central_size = jnp.minimum(2.0 * minmod_size, 0.5 * jnp.abs(left_diff + right_diff))
    superbee_size = jnp.maximum(
        jnp.minimum(2.0 * left_size, right_size), jnp.minimum(left_size, 2.0 * right_size)
    )
    chosen = jnp.where(
        selector == 0.0, minmod_size, jnp.where(selector == 1.0, central_size, superbee_size)
    )
    return agreement * chosen


def advect(padded, selector, courant_row):
    differences = padded[1:] - padded[:-1]
    slopes = limited(differences[:-1], differences[1:], selector[1:-1])
    centers = padded[1:-1]
    forward = courant_row * (centers[:-1] + 0.5 * (1.0 - courant_row) * slopes[:-1])
    backward = courant_row * (centers[1:] - 0.5 * (1.0 + courant_row) * slopes[1:])
    fluxes = jnp.where(courant_row > 0.0, forward, backward)
    return padded[2:-2] - (fluxes[1:] - fluxes[:-1])


def advect_slab(field, selector_padded, courant_part):
    padded = padded_2(field, (("space", 0),), 2)
    return advect(padded, selector_padded, courant_part[None, :])


def heat_all(weight_part, shifted):
    return lax.psum(jnp.dot(shifted, weight_part, precision=highest), ("rows", "cols"))


def swapped(block, axis, distance):
    count = lax.axis_size(axis)
    return lax.ppermute(block, axis, [(i, i ^ distance) for i in range(count)])


def ordered(bit, mine, other):
    first = bit == 0
    return jnp.concatenate(
        [jnp.where(first, mine, other), jnp.where(first, other, mine)], axis=1
    )


def gathered_rows(block, far):
    if lax.axis_size("rows") != 4:
        return lax.all_gather(block, "rows", axis=1, tiled=True)
    row = lax.axis_index("rows")
    near_pair = ordered(row % 2, block, swapped(block, "rows", 1))
    far_pair = ordered(row % 2, far, swapped(far, "rows", 1))
    return ordered(row // 2, near_pair, far_pair)


def gathered_cols(block):
    if lax.axis_size("cols") != 2:
        return lax.all_gather(block, "cols", axis=1, tiled=True)
    return ordered(lax.axis_index("cols"), block, swapped(block, "cols", 1))


def halves(bit, array):
    width = array.shape[1] // 2
    low, high_part = array[:, :width], array[:, width:]
    first = bit == 0
    return jnp.where(first, low, high_part), jnp.where(first, high_part, low)


def chunks_of(array):
    unit = array.shape[0] // sum(CHUNKS)
    edges = [unit * sum(CHUNKS[:i]) for i in range(len(CHUNKS) + 1)]
    return [array[low:top] for low, top in zip(edges[:-1], edges[1:])]


def after(array, earlier):
    if earlier is None:
        return array
    return lax.optimization_barrier((array, earlier))[0]


def chained_sum(mine, leaving, axis, distance, arrived):
    coming = swapped(after(leaving, arrived), axis, distance)
    return mine + coming, coming


def on_device(occupation, propagator, flags_first, flags_second, courant, weights):
    row_count = lax.axis_size("rows")
    col_count = lax.axis_size("cols")
    row_index = lax.axis_index("rows")
    col_index = lax.axis_index("cols")
    local_modes = occupation.shape[0]
    weight_total = jnp.sum(weights)

    def part(array, block, count):
        return lax.dynamic_slice_in_dim(array, block * count, count)

    offset_first = col_index * row_count + row_index
    offset_second = row_index * col_count + col_index
    weight_first = part(weights, offset_first, local_modes)
    courant_first = part(courant, offset_first, local_modes)
    weight_second = part(weights, offset_second, local_modes)
    courant_second = part(courant, offset_second, local_modes)
    selectors = padded_2(
        jnp.stack([flags_first.T, flags_second.T]).astype(jnp.float32), (("space", 1),), 2
    )

    shifted = advect_slab(occupation.T, selectors[0], courant_first)
    heat = (heat_all(weight_first, shifted) / weight_total)[:, None]
    deviation = shifted - heat * weight_first[None, :]
    pieces = chunks_of(deviation)
    fars = []
    for piece in pieces:
        fars.append(swapped(after(piece, fars[-1] if fars else None), "rows", row_count // 2))
    middles = []
    partial = leaving = arrived = None
    for piece, far in zip(pieces, fars):
        block = after(gathered_rows(piece, after(far, partial)), leaving)
        partial = lax.dot_general(
            block,
            propagator,
            (((1,), (1,)), ((), ())),
            precision=high,
            preferred_element_type=jnp.float32,
        )
        if col_count == 2:
            mine, leaving = halves(col_index, partial)
            total, arrived = chained_sum(mine, leaving, "cols", 1, arrived)
            middles.append(total)
        else:
            middles.append(lax.psum_scatter(partial, "cols", scatter_dimension=1, tiled=True))
    middle = jnp.concatenate(middles, axis=0) + heat * weight_second[None, :]

    shifted_second = advect_slab(middle, selectors[1], courant_second)
    heat_second = heat_all(weight_second, shifted_second) / weight_total
    deviation_second = shifted_second - heat_second[:, None] * weight_second[None, :]
    finals = []
    partial = leaving = arrived = None
    for piece in chunks_of(deviation_second):
        block = after(gathered_cols(piece), leaving)
        partial = lax.dot_general(
            block,
            propagator,
            (((1,), (0,)), ((), ())),
            precision=high,
            preferred_element_type=jnp.float32,
        )
        if row_count == 4:
            near, far = halves(row_index // 2, partial)
            far_mine, far_other = halves(row_index % 2, far)
            near_mine, near_other = halves(row_index % 2, near)
            leaving = far_mine + swapped(far_other, "rows", 1)
            mine = near_mine + swapped(near_other, "rows", 1)
            total, arrived = chained_sum(mine, leaving, "rows", 2, arrived)
            finals.append(total)
        else:
            finals.append(lax.psum_scatter(partial, "rows", scatter_dimension=1, tiled=True))
    final = jnp.concatenate(finals, axis=0) + heat_second[:, None] * weight_first[None, :]
    return (final.T, heat_second)


def solution(mesh):
    placed = (
        P(("cols", "rows"), "space"),
        P("rows", "cols"),
        P(("cols", "rows"), "space"),
        P(("rows", "cols"), "space"),
        P(),
        P(),
    )
    return jax.shard_map(
        on_device,
        mesh=mesh,
        in_specs=placed,
        out_specs=(P(("cols", "rows"), "space"), P("space")),
        check_vma=False,
    )
```

time: 711 us -> 509 us (0.72)
  waiting for transfers between devices: 339 us -> 177 us
  matrix products: 263 us -> 176 us
  other arithmetic: 38.7 us -> 65.9 us
  starting transfers between devices: 11.7 us -> 29.6 us
  between operations: 14 us -> 1.69 us
    ppermute x0 -> x16, waiting for transfers between devices: none -> 176 us  [swapped(): return lax.ppermute(block, axis, [(i, i ^ distance) for i in range(count)])]
    reduce_scatter x2 -> x0, waiting for transfers between devices: 170 us -> none  [the longest x1 99.2 us: on_device(): lax.psum_scatter(partial_second, 'rows', scatter_dimension=0, tiled=True)]
    all_gather x2 -> x0, waiting for transfers between devices: 162 us -> none  [the longest x1 81.5 us: on_device(): lax.all_gather(deviation, 'rows', axis=0, tiled=True)]
    dot_general x4 -> x6, matrix products: 263 us -> 176 us  [the longest x2 95.1 us: on_device(): lax.dot_general(block, propagator, (((1,), (0,)), ((), ())), precision=hi...]
    select_n x2 -> x18, other arithmetic: 2.7 us -> 30.6 us  [the longest x8 18.4 us: ordered(): jnp.where(first, mine, other)]
    ppermute x0 -> x16, starting transfers between devices: none -> 11.1 us  [swapped(): return lax.ppermute(block, axis, [(i, i ^ distance) for i in range(count)])]
    ppermute x2 -> x3, starting transfers between devices: 8.32 us -> 14.7 us  [padded_2(): lax.ppermute(lax.slice_in_dim(block, block.shape[dim] - width, None, axis...]
    unnamed x14 -> x44, local copies, waits for them, and re-layouts: 17 us -> 23.2 us
  transfers between devices with their start and end apart: 8 -> 22, of which waited for: 6 -> 9; matrix products, arithmetic and copies ran while one was open for 1% -> 31% of each run, Pallas kernels for 0% -> 0%
where the time goes in v1:
time: 509 us; the launch traced here: 502 us
  waiting for transfers between devices  177 us (35%)
  matrix products  176 us (35%)
  other arithmetic  65.9 us (13%)
  starting transfers between devices  29.6 us (6%)
  blocking collectives  26.9 us (5%)
  local copies, waits for them, and re-layouts  24.7 us (5%)
    ppermute x16, waiting for transfers between devices, swapped(): return lax.ppermute(block, axis, [(i, i ^ distance) for i in range(count)])  176 us
    dot_general x2, matrix products, on_device(): lax.dot_general(block, propagator, (((1,), (0,)), ((), ())), precision=hi...  95.1 us
    dot_general x2, matrix products, on_device(): lax.dot_general(block, propagator, (((1,), (1,)), ((), ())), precision=hi...  74.9 us
    psum x2, blocking collectives, heat_all(): lax.psum(jnp.dot(shifted, weight_part, precision=highest), ('rows', 'cols'))  26.9 us
    unnamed x44, local copies, waits for them, and re-layouts  23.2 us
    select_n x8, other arithmetic, ordered(): jnp.where(first, mine, other)  18.4 us
    ppermute x3, starting transfers between devices, padded_2(): lax.ppermute(lax.slice_in_dim(block, block.shape[dim] - width, None, axis...  14.7 us
    ppermute x16, starting transfers between devices, swapped(): return lax.ppermute(block, axis, [(i, i ^ distance) for i in range(count)])  11.1 us
  transfers between devices with their start and end apart: 22, of which 9 were waited for; matrix products, arithmetic and copies ran while one was open for 31% of the time, Pallas kernels for 0%

profile of v1, /device:TPU:0, one launch (start us, length us, event | category | flops | bytes accessed | tf_op | source)
XLA Modules:
  0.0 502.2 jit_solution(8779965415606199040)
XLA Ops:
  0.6 2.4 copy.8
  4.3 5.6 %collective-permute-start = (f32[2,1536]{1,0:T(2,128)S(1)}, f32[2,1536]{1,0:T(2,128)S(1)}, u32[]{:S(2)}, u32[]{:S(2)}) collective-permute-start(f32[2,1536]{1,0:T(2,128)S(1)} %get-tuple-element.46), channel_id=1, source_target_pairs={{0,8},{8,16},{16,24},{1,9},{9,17},{17,25},{2,10},{10,18},{18,26},{... | collective-permute-start | bytes 36872 | tf_op jit(solution)/shard_map/ppermute | solution.py:16
  9.9 3.5 copy.10
  13.4 3.5 copy.9
  17.0 3.5 add_convert_fusion
  20.5 2.7 copy-done.8
  24.5 4.6 collective-permute-start.2
  34.4 4.0 select_multiply_fusion.1
  39.7 3.1 fusion.27
  42.8 14.2 %psum.14 = f32[512]{0:T(512)S(1)} all-reduce(f32[512]{0:T(512)S(1)} %bitcast.40), channel_id=1, replica_groups=mesh['space'=4,'rows'=4,'cols'=2] {'rows','cols'}, use_global_device_ids=true, to_apply=%region_0.0 | all-reduce | flops 512 | bytes 4096 | tf_op jit(solution)/shard_map/psum | solution.py:55
  57.7 3.5 multiply_subtract_fusion.1
  64.2 3.7 collective-permute-done.8
  67.9 4.9 broadcast_select_fusion.7
  74.4 35.2 %collective-permute-done.5 = f32[256,1536]{1,0:T(8,128)} collective-permute-done((f32[256,1536]{1,0:T(8,128)}, f32[256,1536]{1,0:T(8,128)}, u32[]{:S(2)}, u32[]{:S(2)}) %collective-permute-start.5) | collective-permute-done | bytes 1572896 | tf_op jit(solution)/shard_map/ppermute | solution.py:60
  115.5 3.4 fusion.24
  118.9 37.0 %fusion = f32[256,3072]{1,0:T(8,128)S(1)} fusion(f32[3072,6144]{1,0:T(8,128)} %param.7, f32[256,3072]{1,0:T(8,128)} %get-tuple-element.27, f32[256,3072]{1,0:T(8,128)} %get-tuple-element.26), kind=kOutput, calls=%fused_computation.2 | convolution fusion | flops 28992602112 | bytes 84934656 | tf_op jit(solution)/shard_map/dot_general | solution.py:141
  157.0 2.8 collective-permute-done.10
  162.6 3.1 pad_maximum_fusion.1
  165.7 37.9 %fusion.35 = f32[256,3072]{1,0:T(8,128)} fusion(f32[256,6144]{1,0:T(8,128)} %pad_maximum_fusion.1, f32[3072,6144]{1,0:T(8,128)} %param.7), kind=kOutput, calls=%fused_computation.97 | convolution fusion | flops 28991029248 | bytes 84934656 | tf_op jit(solution)/shard_map/dot_general | solution.py:141
  208.4 33.8 %collective-permute-done.11 = f32[256,1536]{1,0:T(8,128)S(1)} collective-permute-done((f32[256,1536]{1,0:T(8,128)S(1)}, f32[256,1536]{1,0:T(8,128)S(1)}, u32[]{:S(2)}, u32[]{:S(2)}) %collective-permute-start.11) | collective-permute-done | bytes 1572896 | tf_op jit(solution)/shard_map/ppermute | solution.py:60
  244.3 4.5 collective-permute-start.12
  253.2 3.9 select_multiply_fusion
  258.4 3.1 fusion.29
  261.5 12.6 %psum.15 = f32[512]{0:T(512)S(1)} all-reduce(f32[512]{0:T(512)S(1)} %bitcast.41), channel_id=1, replica_groups=mesh['space'=4,'rows'=4,'cols'=2] {'rows','cols'}, use_global_device_ids=true, to_apply=%region_2.3 | all-reduce | flops 512 | bytes 4096 | tf_op jit(solution)/shard_map/psum | solution.py:55
  274.8 3.5 multiply_subtract_fusion
  280.3 34.6 %collective-permute-done.14 = f32[256,1536]{1,0:T(8,128)S(1)} collective-permute-done((f32[256,1536]{1,0:T(8,128)S(1)}, f32[256,1536]{1,0:T(8,128)S(1)}, u32[]{:S(2)}, u32[]{:S(2)}) %collective-permute-start.14) | collective-permute-done | bytes 1572896 | tf_op jit(solution)/shard_map/ppermute | solution.py:60
  317.6 42.6 %fusion.16 = f32[256,6144]{1,0:T(8,128)} fusion(f32[3072,6144]{1,0:T(8,128)} %param.7, f32[256,1536]{1,0:T(8,128)S(1)} %get-tuple-element.31, f32[256,1536]{1,0:T(8,128)S(1)} %get-tuple-element.30), kind=kOutput, calls=%fused_computation.40 | convolution fusion | flops 28991815680 | bytes 84934656 | tf_op jit(solution)/shard_map/dot_general | solution.py:163
  360.3 3.3 slice_select_fusion.3
  370.6 52.5 %fusion.36 = f32[256,6144]{1,0:T(8,128)} fusion(f32[256,3072]{1,0:T(8,128)} %pad_maximum_fusion.12, f32[3072,6144]{1,0:T(8,128)} %param.7), kind=kOutput, calls=%fused_computation.98 | convolution fusion | flops 28991029248 | bytes 84934656 | tf_op jit(solution)/shard_map/dot_general | solution.py:163
  423.1 3.3 slice_select_fusion.1
  430.9 32.7 %collective-permute-done.17 = f32[256,1536]{1,0:T(8,128)S(1)} collective-permute-done((f32[256,1536]{1,0:T(8,128)S(1)}, f32[256,1536]{1,0:T(8,128)S(1)}, u32[]{:S(2)}, u32[]{:S(2)}) %collective-permute-start.17) | collective-permute-done | bytes 1572896 | tf_op jit(solution)/shard_map/ppermute | solution.py:60
  465.7 32.6 %collective-permute-done.21 = f32[256,1536]{1,0:T(8,128)S(1)} collective-permute-done((f32[256,1536]{1,0:T(8,128)S(1)}, f32[256,1536]{1,0:T(8,128)S(1)}, u32[]{:S(2)}, u32[]{:S(2)}) %collective-permute-start.21) | collective-permute-done | bytes 1572896 | tf_op jit(solution)/shard_map/ppermute | solution.py:60
  (118 shorter events, 58.8 us)
Async XLA Ops:
  3.0 27.6 %collective-permute-start.1 = (f32[2,1536]{1,0:T(2,128)S(1)}, f32[2,1536]{1,0:T(2,128)S(1)}, u32[]{:S(2)}, u32[]{:S(2)}) collective-permute-start(f32[2,1536]{1,0:T(2,128)S(1)} %get-tuple-element.47), channel_id=1, source_target_pairs={{8,0},{16,8},{24,16},{9,1},{17,9},{25,17},{10,2},{18,10},{26,18},{... | collective-permute-start | bytes 36872 | tf_op jit(solution)/shard_map/ppermute | solution.py:19
  4.3 26.3 %collective-permute-start = (f32[2,1536]{1,0:T(2,128)S(1)}, f32[2,1536]{1,0:T(2,128)S(1)}, u32[]{:S(2)}, u32[]{:S(2)}) collective-permute-start(f32[2,1536]{1,0:T(2,128)S(1)} %get-tuple-element.46), channel_id=1, source_target_pairs={{0,8},{8,16},{16,24},{1,9},{9,17},{17,25},{2,10},{10,18},{18,26},{... | collective-permute-start | bytes 36872 | tf_op jit(solution)/shard_map/ppermute | solution.py:16
  17.0 13.0 %copy-start.14 = (f32[12288]{0:T(1024)S(1)}, f32[12288]{0:T(1024)}, u32[]{:S(2)}) copy-start(f32[12288]{0:T(1024)} %param.11) | copy-start | bytes 147460
  23.2 8.3 %collective-permute-start.3 = (f32[2,2,1536]{2,1,0:T(2,128)S(1)}, f32[2,2,1536]{2,1,0:T(2,128)S(1)}, u32[]{:S(2)}, u32[]{:S(2)}) collective-permute-start(f32[2,2,1536]{2,1,0:T(2,128)S(1)} %get-tuple-element.29), channel_id=1, source_target_pairs={{8,0},{16,8},{24,16},{9,1},{17,9},{25,17},{10,2},{18,10},{26,18},{... | collective-permute-start | bytes 73736 | tf_op jit(solution)/shard_map/ppermute | solution.py:19
  24.5 7.0 %collective-permute-start.2 = (f32[2,2,1536]{2,1,0:T(2,128)S(1)}, f32[2,2,1536]{2,1,0:T(2,128)S(1)}, u32[]{:S(2)}, u32[]{:S(2)}) collective-permute-start(f32[2,2,1536]{2,1,0:T(2,128)S(1)} %get-tuple-element.28), channel_id=1, source_target_pairs={{0,8},{8,16},{16,24},{1,9},{9,17},{17,25},{2,10},{10,18},{18,26},{... | collective-permute-start | bytes 73736 | tf_op jit(solution)/shard_map/ppermute | solution.py:16
  30.0 27.7 %copy-start.12 = (f32[1536]{0:T(1024)}, f32[1536]{0:T(1024)S(1)}, u32[]{:S(2)}) copy-start(f32[1536]{0:T(1024)S(1)} %get-tuple-element.50) | copy-start | bytes 18436
  34.4 4.0 copy-start.7
  64.2 3.8 collective-permute-start.8
  64.2 47.0 %copy-start.4 = (f32[512,1536]{1,0:T(8,128)S(1)}, f32[512,1536]{1,0:T(8,128)}, u32[]{:S(2)}) copy-start(f32[512,1536]{1,0:T(8,128)} %copy-done.3) | copy-start | bytes 9437188
  72.8 36.8 %collective-permute-start.5 = (f32[256,1536]{1,0:T(8,128)}, f32[256,1536]{1,0:T(8,128)}, u32[]{:S(2)}, u32[]{:S(2)}) collective-permute-start(f32[256,1536]{1,0:T(8,128)} %get-tuple-element.41), channel_id=1, source_target_pairs={{0,4},{2,6},{4,0},{6,2},{1,5},{3,7},{5,1},{7,3},{8,12},{10,14},{12... | collective-permute-start | bytes 4718600 | tf_op jit(solution)/shard_map/ppermute | solution.py:60
  74.4 36.8 %collective-permute-start.4 = (f32[256,1536]{1,0:T(8,128)}, f32[256,1536]{1,0:T(8,128)}, u32[]{:S(2)}, u32[]{:S(2)}) collective-permute-start(f32[256,1536]{1,0:T(8,128)} %get-tuple-element.41), channel_id=1, source_target_pairs={{0,2},{2,0},{4,6},{6,4},{1,3},{3,1},{5,7},{7,5},{8,10},{10,8},{12,... | collective-permute-start | bytes 4718600 | tf_op jit(solution)/shard_map/ppermute | solution.py:60
  109.6 3.8 collective-permute-start.6
  109.6 46.3 %collective-permute-start.9 = (f32[256,1536]{1,0:T(8,128)}, f32[256,1536]{1,0:T(8,128)}, u32[]{:S(2)}, u32[]{:S(2)}) collective-permute-start(f32[256,1536]{1,0:T(8,128)} %slice.224), channel_id=1, source_target_pairs={{0,4},{2,6},{4,0},{6,2},{1,5},{3,7},{5,1},{7,3},{8,12},{10,14},{12... | collective-permute-start | bytes 4718600 | tf_op jit(solution)/shard_map/ppermute | solution.py:60
  155.9 3.8 collective-permute-start.10
  156.3 5.6 %copy-start.9 = (f32[256,1536]{1,0:T(8,128)S(1)}, f32[256,1536]{1,0:T(8,128)}, u32[]{:S(2)}) copy-start(f32[256,1536]{1,0:T(8,128)} %get-tuple-element.34) | copy-start | bytes 4718596
  156.4 5.6 %copy-start.10 = (f32[256,1536]{1,0:T(8,128)S(1)}, f32[256,1536]{1,0:T(8,128)}, u32[]{:S(2)}) copy-start(f32[256,1536]{1,0:T(8,128)} %get-tuple-element.35) | copy-start | bytes 4718596
  156.4 49.4 %collective-permute-start.7 = (f32[256,1536]{1,0:T(8,128)S(1)}, f32[256,1536]{1,0:T(8,128)}, u32[]{:S(2)}, u32[]{:S(2)}) collective-permute-start(f32[256,1536]{1,0:T(8,128)S(1)} %slice_select_fusion.9), channel_id=1, source_target_pairs={{0,1},{1,0},{2,3},{3,2},{4,5},{5,4},{6,7},{7,6},{8,9},{9,8},{10,11... | collective-permute-start | bytes 4718600 | tf_op jit(solution)/shard_map/ppermute | solution.py:60
  205.7 36.5 %copy-start.2 = (f32[256,3072]{1,0:T(8,128)S(1)}, f32[256,3072]{1,0:T(8,128)}, u32[]{:S(2)}) copy-start(f32[256,3072]{1,0:T(8,128)} %fusion.35) | copy-start | bytes 9437188
  205.7 36.5 %collective-permute-start.11 = (f32[256,1536]{1,0:T(8,128)S(1)}, f32[256,1536]{1,0:T(8,128)S(1)}, u32[]{:S(2)}, u32[]{:S(2)}) collective-permute-start(f32[256,1536]{1,0:T(8,128)S(1)} %slice_select_fusion.8), channel_id=1, source_target_pairs={{0,1},{1,0},{2,3},{3,2},{4,5},{5,4},{6,7},{7,6},{8,9},{9,8},{10,11... | collective-permute-start | bytes 4718600 | tf_op jit(solution)/shard_map/ppermute | solution.py:60
  243.0 5.9 %collective-permute-start.13 = (f32[2,1536]{1,0:T(2,128)S(1)}, f32[2,1536]{1,0:T(2,128)S(1)}, u32[]{:S(2)}, u32[]{:S(2)}) collective-permute-start(f32[2,1536]{1,0:T(2,128)S(1)} %get-tuple-element.40), channel_id=1, source_target_pairs={{8,0},{16,8},{24,16},{9,1},{17,9},{25,17},{10,2},{18,10},{26,18},{... | collective-permute-start | bytes 36872 | tf_op jit(solution)/shard_map/ppermute | solution.py:19
  244.3 5.9 %collective-permute-start.12 = (f32[2,1536]{1,0:T(2,128)S(1)}, f32[2,1536]{1,0:T(2,128)S(1)}, u32[]{:S(2)}, u32[]{:S(2)}) collective-permute-start(f32[2,1536]{1,0:T(2,128)S(1)} %get-tuple-element.39), channel_id=1, source_target_pairs={{0,8},{8,16},{16,24},{1,9},{9,17},{17,25},{2,10},{10,18},{18,26},{... | collective-permute-start | bytes 36872 | tf_op jit(solution)/shard_map/ppermute | solution.py:16
  274.8 224.2 %copy-start.15 = (f32[512]{0:T(512)}, f32[512]{0:T(512)S(1)}, u32[]{:S(2)}) copy-start(f32[512]{0:T(512)S(1)} %broadcast_divide_fusion) | copy-start | bytes 6148
  278.4 38.3 %copy-start.5 = (f32[512,1536]{1,0:T(8,128)}, f32[512,1536]{1,0:T(8,128)S(1)}, u32[]{:S(2)}) copy-start(f32[512,1536]{1,0:T(8,128)S(1)} %multiply_subtract_fusion) | copy-start | bytes 9437188
  278.5 36.4 %collective-permute-start.14 = (f32[256,1536]{1,0:T(8,128)S(1)}, f32[256,1536]{1,0:T(8,128)S(1)}, u32[]{:S(2)}, u32[]{:S(2)}) collective-permute-start(f32[256,1536]{1,0:T(8,128)S(1)} %slice.238), channel_id=1, source_target_pairs={{0,1},{1,0},{2,3},{3,2},{4,5},{5,4},{6,7},{7,6},{8,9},{9,8},{10,11... | collective-permute-start | bytes 4718600 | tf_op jit(solution)/shard_map/ppermute | solution.py:60
  316.7 47.2 %collective-permute-start.18 = (f32[256,1536]{1,0:T(8,128)}, f32[256,1536]{1,0:T(8,128)}, u32[]{:S(2)}, u32[]{:S(2)}) collective-permute-start(f32[256,1536]{1,0:T(8,128)} %get-tuple-element.38), channel_id=1, source_target_pairs={{0,1},{1,0},{2,3},{3,2},{4,5},{5,4},{6,7},{7,6},{8,9},{9,8},{10,11... | collective-permute-start | bytes 4718600 | tf_op jit(solution)/shard_map/ppermute | solution.py:60
  363.8 5.3 %collective-permute-start.16 = (f32[256,1536]{1,0:T(8,128)S(1)}, f32[256,1536]{1,0:T(8,128)S(1)}, u32[]{:S(2)}, u32[]{:S(2)}) collective-permute-start(f32[256,1536]{1,0:T(8,128)S(1)} %slice_select_fusion.6), channel_id=1, source_target_pairs={{0,2},{2,0},{4,6},{6,4},{1,3},{3,1},{5,7},{7,5},{8,10},{10,8},{12,... | collective-permute-start | bytes 4718600 | tf_op jit(solution)/shard_map/ppermute | solution.py:60
  426.7 3.8 collective-permute-start.20
  427.8 35.7 %collective-permute-start.17 = (f32[256,1536]{1,0:T(8,128)S(1)}, f32[256,1536]{1,0:T(8,128)S(1)}, u32[]{:S(2)}, u32[]{:S(2)}) collective-permute-start(f32[256,1536]{1,0:T(8,128)S(1)} %copy-done.11), channel_id=1, source_target_pairs={{0,4},{2,6},{4,0},{6,2},{1,5},{3,7},{5,1},{7,3},{8,12},{10,14},{12... | collective-permute-start | bytes 4718600 | tf_op jit(solution)/shard_map/ppermute | solution.py:60
  429.6 35.5 %collective-permute-start.15 = (f32[256,1536]{1,0:T(8,128)S(1)}, f32[256,1536]{1,0:T(8,128)S(1)}, u32[]{:S(2)}, u32[]{:S(2)}) collective-permute-start(f32[256,1536]{1,0:T(8,128)S(1)} %slice_select_fusion.7), channel_id=1, source_target_pairs={{0,2},{2,0},{4,6},{6,4},{1,3},{3,1},{5,7},{7,5},{8,10},{10,8},{12,... | collective-permute-start | bytes 4718600 | tf_op jit(solution)/shard_map/ppermute | solution.py:60
  429.8 35.9 %collective-permute-start.19 = (f32[256,1536]{1,0:T(8,128)S(1)}, f32[256,1536]{1,0:T(8,128)S(1)}, u32[]{:S(2)}, u32[]{:S(2)}) collective-permute-start(f32[256,1536]{1,0:T(8,128)S(1)} %slice_select_fusion.5), channel_id=1, source_target_pairs={{0,2},{2,0},{4,6},{6,4},{1,3},{3,1},{5,7},{7,5},{8,10},{10,8},{12,... | collective-permute-start | bytes 4718600 | tf_op jit(solution)/shard_map/ppermute | solution.py:60
  463.5 34.8 %collective-permute-start.21 = (f32[256,1536]{1,0:T(8,128)S(1)}, f32[256,1536]{1,0:T(8,128)S(1)}, u32[]{:S(2)}, u32[]{:S(2)}) collective-permute-start(f32[256,1536]{1,0:T(8,128)S(1)} %select_add_fusion), channel_id=1, source_target_pairs={{0,4},{2,6},{4,0},{6,2},{1,5},{3,7},{5,1},{7,3},{8,12},{10,14},{12... | collective-permute-start | bytes 4718600 | tf_op jit(solution)/shard_map/ppermute | solution.py:60
  465.7 33.3 %copy-start.13 = (f32[1536]{0:T(1024)S(1)}, f32[1536]{0:T(1024)}, u32[]{:S(2)}) copy-start(f32[1536]{0:T(1024)} %copy-done.12) | copy-start | bytes 18436
  (10 other events, 23.5 us)
